TPU v7x, 256 devices: a whole 4x4x8 slice. The times are simulated.
256 devices in a mesh: depth: 32 (over x, y, core), tile: 8 (over z).
Axes of the slice: x: 4, y: 4, z: 8, core: 2. Of those that a mesh axis runs over, the one named last changes fastest.
Arguments:
- fronts: float32 [32, 8, 8, 2, 128, 128], P('depth', 'tile'), may hold values from -6 to 6
- probe_wave: float32 [2, 128, 128], replicated, may hold values from -6 to 6
- object_slices: bfloat16 [64, 2, 3072, 384], P('depth', None, 'tile')
- patch_list: int32 [35, 8, 3, 8], P(None, 'tile'), may hold values from 0 to 256, as said below
- counts: int32 [35, 8], P(None, 'tile'), may hold values from 1 to 8, as said below
Outputs:
- exit_waves: float32 [32, 8, 8, 2, 128, 128], P('depth', 'tile')
Inputs may be any that keep to these rules, and one draw needn't show every extreme that they name: `patch_list`: rows and columns of corners run from 0 to 256, and that end is reached. Among the live probes of one batch of one owner no tile is named more than 1 times; a batch of 8 probes names every tile exactly 1 times. `counts`: some batch of some owner holds 8 probes.
All inputs are finite; a program needn't handle non-finite values.
Results may differ from a plain program's by a relative error of at most 0.0003.
Values may be sent and summed in bfloat16 or wider, within the bound.
A program may use at most 64 MiB of HBM per device.

v0:
```python
import math
import jax
import jax.numpy as jnp
from jax import lax
from jax.sharding import PartitionSpec as P

STEPS = 4
fresnel_rate = 0.3


def from_behind(value, axis, steps):
    count = lax.axis_size(axis)
    leading, last = (max(0, -steps), min(count, count - steps))
    return lax.ppermute(value, axis, [(source, source + steps) for source in range(leading, last)])


def dft_tables(width, inverse):
    index = jnp.arange(width, dtype=jnp.int32)
    angle = 2.0 * math.pi / width * (index[:, None] * index[None, :] % width).astype(jnp.float32)
    cosine = jnp.cos(angle)
    sine = jnp.sin(angle)
    if inverse:
        cosine = cosine / width
        imagine = sine / width
    else:
        imagine = -sine
    return (cosine, cosine + imagine, imagine - cosine)


def plane_dot(plane, table):
    shape = plane.shape
    flat = plane.reshape(-1, shape[-1])
    return jnp.dot(
        flat, table, precision=lax.Precision.HIGHEST, preferred_element_type=jnp.float32
    ).reshape(shape)


def right_multiply(real_part, imag_part, tables):
    cosine, summed, differ = tables
    first = plane_dot(real_part + imag_part, cosine)
    second = plane_dot(real_part, differ)
    third = plane_dot(imag_part, summed)
    return (first - third, first + second)


def transform(real_part, imag_part, tables):
    real_part, imag_part = right_multiply(real_part, imag_part, tables)
    return right_multiply(jnp.swapaxes(real_part, -1, -2), jnp.swapaxes(imag_part, -1, -2), tables)


def fresnel(width):
    index = jnp.arange(width, dtype=jnp.int32)
    freq = jnp.where(index < width // 2, index, index - width).astype(jnp.float32)
    phase = -2.0 * math.pi * fresnel_rate / width * (freq[:, None] ** 2 + freq[None, :] ** 2)
    return (jnp.cos(phase), jnp.sin(phase))


def slab_pass(wavefield, patches):
    width = wavefield.shape[-1]
    forward = dft_tables(width, False)
    backward = dft_tables(width, True)
    kernel_cos, kernel_sin = fresnel(width)
    real_part = wavefield[:, 0]
    imag_part = wavefield[:, 1]
    for layer in range(2):
        trans_real = patches[:, layer, 0].astype(jnp.float32)
        trans_imag = patches[:, layer, 1].astype(jnp.float32)
        real_part, imag_part = (
            real_part * trans_real - imag_part * trans_imag,
            real_part * trans_imag + imag_part * trans_real,
        )
        spec_real, spec_imag = transform(real_part, imag_part, forward)
        spec_real, spec_imag = (
            spec_real * kernel_cos - spec_imag * kernel_sin,
            spec_real * kernel_sin + spec_imag * kernel_cos,
        )
        real_part, imag_part = transform(spec_real, spec_imag, backward)
    return jnp.stack([real_part, imag_part], axis=1)


def rank_within(tile_ids, live):
    slot_index = jnp.arange(tile_ids.shape[0], dtype=jnp.int32)
    same = (
        (tile_ids[:, None] == tile_ids[None, :])
        & live[None, :]
        & (slot_index[None, :] < slot_index[:, None])
    )
    return jnp.sum(same.astype(jnp.int32), axis=1)


def cut_from(source, row_value, column_value, width):
    zero = jnp.zeros((), jnp.int32)
    return lax.dynamic_slice(source, (zero, zero, row_value, column_value), (2, 2, width, width))


def per_device(fronts, probe_wave, object_slices, patch_list, counts):
    depth_count = lax.axis_size("depth")
    tile_count = lax.axis_size("tile")
    depth_index = lax.axis_index("depth")
    tile_index = lax.axis_index("tile")
    slots = fronts.shape[2]
    width = fronts.shape[-1]
    pair = slots // tile_count
    slot_index = jnp.arange(slots, dtype=jnp.int32)
    own_lists = patch_list[:, 0]
    own_counts = counts[:, 0]
    batch_ids = [step + depth_count - 1 - depth_index for step in range(STEPS)]
    step_lists = jnp.stack(
        [lax.dynamic_index_in_dim(own_lists, batch, 0, keepdims=False) for batch in batch_ids]
    )
    step_counts = jnp.stack(
        [lax.dynamic_index_in_dim(own_counts, batch, 0, keepdims=False) for batch in batch_ids]
    )

    def outgoing(all_lists, all_counts):
        tile_ids = all_lists[:, 0]
        live = slot_index[None, :] < all_counts[:, None]
        order = jax.vmap(rank_within)(tile_ids, live)
        target = live & (tile_ids == tile_index)
        choose = (
            target[:, None, :]
            & (order[:, None, :] == jnp.arange(pair, dtype=jnp.int32)[None, :, None])
        ).astype(jnp.int32)
        row_start = jnp.sum(choose * all_lists[:, 1][:, None, :], axis=-1)
        column_start = jnp.sum(choose * all_lists[:, 2][:, None, :], axis=-1)
        valid = jnp.sum(choose, axis=-1) > 0

        def cut_local(row_value, column_value):
            return cut_from(object_slices, row_value, column_value, width)

        cuts = jax.vmap(jax.vmap(cut_local))(row_start, column_start)
        return jnp.where(valid[:, :, None, None, None, None], cuts, jnp.zeros_like(cuts))

    wavefield = fronts[0, 0]
    for step in range(STEPS):
        listing = step_lists[step]
        count = step_counts[step]
        live = (slot_index < count).astype(jnp.float32)[:, None, None, None]
        if step > 0:
            arrived = from_behind(wavefield, "depth", 1)
            wavefield = jnp.where(depth_index == 0, probe_wave[None] * live, arrived)
        else:
            wavefield = wavefield * live
        got_lists, got_counts = (
            lax.all_gather(listing[None], "tile", axis=0, tiled=True),
            lax.all_gather(count[None], "tile", axis=0, tiled=True),
        )
        received = lax.all_to_all(
            outgoing(got_lists, got_counts), "tile", split_axis=0, concat_axis=0, tiled=True
        )
        incoming_tile_ids = listing[0]
        incoming_live = slot_index < count
        incoming_order = rank_within(incoming_tile_ids, incoming_live)
        place = incoming_tile_ids * pair + jnp.minimum(incoming_order, pair - 1)
        flat = received.reshape((tile_count * pair,) + received.shape[2:])
        patches = jnp.take(flat, place, axis=0)
        wavefield = slab_pass(wavefield, patches)
    return wavefield[None, None]


def solution(mesh):
    in_specs = (
        P("depth", "tile", None, None, None, None),
        P(),
        P("depth", None, "tile", None),
        P(None, "tile", None, None),
        P(None, "tile"),
    )
    out_specs = P("depth", "tile", None, None, None, None)
    return jax.shard_map(
        per_device, mesh=mesh, in_specs=in_specs, out_specs=out_specs, check_vma=False
    )
```

profile of v0, /device:TPU:38, one launch (start us, length us, event | category | flops | bytes accessed | tf_op | source)
XLA Modules:
  0.0 397.6 jit_solution(2629929279038056412)
XLA Ops:
  7.9 15.2 %all-reduce.4 = (s32[8]{0:T(128)S(1)}, s32[8]{0:T(128)S(1)}, s32[8]{0:T(128)S(1)}, s32[8]{0:T(128)S(1)}) all-reduce(s32[8]{0:T(128)S(1)} %bitcast_dynamic-update-slice_fusion.4, s32[8]{0:T(128)S(1)} %bitcast_dynamic-update-slice_fusion.5, s32[8]{0:T(128)S(1)} %bitcast_dynamic-update-slice_fusion.6, ...), channel_id=8, replica_groups=mesh['depth'=32,'tile'=8] {'tile'}, use_global_device_ids=true, to_apply=%add.3 | all-reduce | flops 32 | bytes 256 | tf_op jit(solution)/shard_map/all_gather | solution.py:146
  24.5 20.8 %all-gather.7 = s32[8,1,3,8]{3,1,2,0:T(1,128)S(1)} all-gather(s32[1,1,3,8]{3,1,2,0:T(1,128)S(1)} %copy.293), channel_id=9, replica_groups=mesh['depth'=32,'tile'=8] {'tile'}, dimensions={0}, use_global_device_ids=true | all-gather | bytes 864 | tf_op jit(solution)/shard_map/all_gather | solution.py:145
  45.4 20.7 %all-gather.5 = s32[8,1,3,8]{3,1,2,0:T(1,128)S(1)} all-gather(s32[1,1,3,8]{3,1,2,0:T(1,128)S(1)} %copy.292), channel_id=7, replica_groups=mesh['depth'=32,'tile'=8] {'tile'}, dimensions={0}, use_global_device_ids=true | all-gather | bytes 864 | tf_op jit(solution)/shard_map/all_gather | solution.py:145
  66.2 20.7 %all-gather.3 = s32[8,1,3,8]{3,1,2,0:T(1,128)S(1)} all-gather(s32[1,1,3,8]{3,1,2,0:T(1,128)S(1)} %copy.291), channel_id=5, replica_groups=mesh['depth'=32,'tile'=8] {'tile'}, dimensions={0}, use_global_device_ids=true | all-gather | bytes 864 | tf_op jit(solution)/shard_map/all_gather | solution.py:145
  87.0 21.1 %all-gather.1 = s32[8,1,3,8]{3,1,2,0:T(1,128)S(1)} all-gather(s32[1,1,3,8]{3,1,2,0:T(1,128)S(1)} %copy.290), channel_id=3, replica_groups=mesh['depth'=32,'tile'=8] {'tile'}, dimensions={0}, use_global_device_ids=true | all-gather | bytes 864 | tf_op jit(solution)/shard_map/all_gather | solution.py:145
  110.1 24.6 %while.4 = (s32[]{:T(128)}, bf16[2,2,384,384]{3,2,1,0:T(8,128)(2,1)}, s32[8,4]{0,1:T(4,128)S(1)}, bf16[8,2,2,128,128]{4,3,2,1,0:T(8,128)(2,1)S(1)}, s32[]{:T(128)}) while((s32[]{:T(128)}, bf16[2,2,384,384]{3,2,1,0:T(8,128)(2,1)}, s32[8,4]{0,1:T(4,128)S(1)}, bf16[8,2,2,128,128]{4,3,2,1,0:T(8,128)(2,1)S(1)}, s32[]{:T(128)}) %tuple.93), condition=%wide.while_cond, body=%wide.while_body.sunk | while | flops 2 | bytes 262269 | solution.py:93
  110.8 2.4 bitcast_dynamic-update-slice_fusion.12
  113.9 2.4 bitcast_dynamic-update-slice_fusion.12
  116.9 2.4 bitcast_dynamic-update-slice_fusion.12
  120.0 2.4 bitcast_dynamic-update-slice_fusion.12
  123.1 2.4 bitcast_dynamic-update-slice_fusion.12
  126.2 2.4 bitcast_dynamic-update-slice_fusion.12
  129.2 2.4 bitcast_dynamic-update-slice_fusion.12
  132.3 2.4 bitcast_dynamic-update-slice_fusion.12
  135.9 6.2 %all-to-all-start = ((bf16[8,1,2,2,128,128]{5,4,3,2,1,0:T(8,128)(2,1)}), bf16[8,1,2,2,128,128]{5,4,3,2,1,0:T(8,128)(2,1)S(1)}, u32[]{:S(2)}, u32[]{:S(2)}) async-start(bf16[8,1,2,2,128,128]{5,4,3,2,1,0:T(8,128)(2,1)} %bitcast_select_fusion.3), calls=%async_computation | async-start | bytes 2097152 | tf_op jit(solution)/shard_map/all_to_all | solution.py:148
  145.4 24.1 %while.5 = (s32[]{:T(128)}, bf16[2,2,384,384]{3,2,1,0:T(8,128)(2,1)}, s32[8,4]{0,1:T(4,128)S(1)}, bf16[8,2,2,128,128]{4,3,2,1,0:T(8,128)(2,1)S(1)}, s32[]{:T(128)}) while((s32[]{:T(128)}, bf16[2,2,384,384]{3,2,1,0:T(8,128)(2,1)}, s32[8,4]{0,1:T(4,128)S(1)}, bf16[8,2,2,128,128]{4,3,2,1,0:T(8,128)(2,1)S(1)}, s32[]{:T(128)}) %tuple.105), condition=%wide.while_cond.1, body=%wide.while_body.1.sunk | while | flops 2 | bytes 262269 | solution.py:93
  146.1 2.3 bitcast_dynamic-update-slice_fusion.13
  149.1 2.3 bitcast_dynamic-update-slice_fusion.13
  152.1 2.3 bitcast_dynamic-update-slice_fusion.13
  155.1 2.3 bitcast_dynamic-update-slice_fusion.13
  158.1 2.3 bitcast_dynamic-update-slice_fusion.13
  161.1 2.3 bitcast_dynamic-update-slice_fusion.13
  164.1 2.3 bitcast_dynamic-update-slice_fusion.13
  167.1 2.3 bitcast_dynamic-update-slice_fusion.13
  171.6 29.4 %while.6 = (s32[]{:T(128)}, bf16[2,2,384,384]{3,2,1,0:T(8,128)(2,1)}, s32[8,4]{0,1:T(4,128)S(1)}, bf16[8,2,2,128,128]{4,3,2,1,0:T(8,128)(2,1)}, s32[]{:T(128)}) while((s32[]{:T(128)}, bf16[2,2,384,384]{3,2,1,0:T(8,128)(2,1)}, s32[8,4]{0,1:T(4,128)S(1)}, bf16[8,2,2,128,128]{4,3,2,1,0:T(8,128)(2,1)}, s32[]{:T(128)}) %tuple.106), condition=%wide.while_cond.2, body=%wide.while_body.2.sunk | while | flops 2 | bytes 263793 | solution.py:93
  172.2 3.0 bitcast_dynamic-update-slice_fusion.14
  175.9 3.0 bitcast_dynamic-update-slice_fusion.14
  179.6 3.0 bitcast_dynamic-update-slice_fusion.14
  183.3 3.0 bitcast_dynamic-update-slice_fusion.14
  186.9 3.0 bitcast_dynamic-update-slice_fusion.14
  190.6 3.0 bitcast_dynamic-update-slice_fusion.14
  194.3 3.0 bitcast_dynamic-update-slice_fusion.14
  198.0 3.0 bitcast_dynamic-update-slice_fusion.14
  203.8 23.7 %while.7 = (s32[]{:T(128)}, bf16[2,2,384,384]{3,2,1,0:T(8,128)(2,1)}, s32[8,4]{0,1:T(4,128)S(1)}, bf16[8,2,2,128,128]{4,3,2,1,0:T(8,128)(2,1)S(1)}, s32[]{:T(128)}) while((s32[]{:T(128)}, bf16[2,2,384,384]{3,2,1,0:T(8,128)(2,1)}, s32[8,4]{0,1:T(4,128)S(1)}, bf16[8,2,2,128,128]{4,3,2,1,0:T(8,128)(2,1)S(1)}, s32[]{:T(128)}) %tuple.107), condition=%wide.while_cond.3, body=%wide.while_body.3.sunk | while | flops 2 | bytes 262269 | solution.py:93
  204.4 2.3 bitcast_dynamic-update-slice_fusion.15
  207.4 2.3 bitcast_dynamic-update-slice_fusion.15
  210.3 2.3 bitcast_dynamic-update-slice_fusion.15
  213.3 2.3 bitcast_dynamic-update-slice_fusion.15
  216.3 2.3 bitcast_dynamic-update-slice_fusion.15
  219.2 2.3 bitcast_dynamic-update-slice_fusion.15
  222.2 2.3 bitcast_dynamic-update-slice_fusion.15
  227.5 7.4 %all-to-all-start.1 = ((bf16[8,1,2,2,128,128]{5,4,3,2,1,0:T(8,128)(2,1)}), bf16[8,1,2,2,128,128]{5,4,3,2,1,0:T(8,128)(2,1)}, u32[]{:S(2)}, u32[]{:S(2)}) async-start(bf16[8,1,2,2,128,128]{5,4,3,2,1,0:T(8,128)(2,1)} %bitcast_select_fusion.2), calls=%async_computation.1 | async-start | bytes 2097152 | tf_op jit(solution)/shard_map/all_to_all | solution.py:148
  263.6 2.3 bitcast_select_fusion.1
  266.0 7.2 %all-to-all-start.2 = ((bf16[8,1,2,2,128,128]{5,4,3,2,1,0:T(8,128)(2,1)}), bf16[8,1,2,2,128,128]{5,4,3,2,1,0:T(8,128)(2,1)S(1)}, u32[]{:S(2)}, u32[]{:S(2)}) async-start(bf16[8,1,2,2,128,128]{5,4,3,2,1,0:T(8,128)(2,1)} %bitcast_select_fusion.1), calls=%async_computation.2 | async-start | bytes 2097152 | tf_op jit(solution)/shard_map/all_to_all | solution.py:148
  275.3 4.0 %collective-permute-done = f32[8,2,128,128]{3,2,0,1:T(8,128)} collective-permute-done((f32[8,2,128,128]{3,2,0,1:T(8,128)S(1)}, f32[8,2,128,128]{3,2,0,1:T(8,128)}, u32[]{:S(2)}, u32[]{:S(2)}) %collective-permute-start) | collective-permute-done | bytes 1048608 | tf_op jit(solution)/shard_map/ppermute | solution.py:14
  310.8 7.2 %all-to-all-start.3 = ((bf16[8,1,2,2,128,128]{5,4,3,2,1,0:T(8,128)(2,1)}), bf16[8,1,2,2,128,128]{5,4,3,2,1,0:T(8,128)(2,1)S(1)}, u32[]{:S(2)}, u32[]{:S(2)}) async-start(bf16[8,1,2,2,128,128]{5,4,3,2,1,0:T(8,128)(2,1)} %bitcast_select_fusion), calls=%async_computation.3 | async-start | bytes 2097152 | tf_op jit(solution)/shard_map/all_to_all | solution.py:148
  318.9 6.5 %collective-permute-done.1 = f32[8,2,128,128]{3,2,0,1:T(8,128)} collective-permute-done((f32[8,2,128,128]{3,2,0,1:T(8,128)}, f32[8,2,128,128]{3,2,0,1:T(8,128)}, u32[]{:S(2)}, u32[]{:S(2)}) %collective-permute-start.1) | collective-permute-done | bytes 1048608 | tf_op jit(solution)/shard_map/ppermute | solution.py:14
  356.6 14.8 %collective-permute-done.2 = f32[8,2,128,128]{3,2,0,1:T(8,128)S(1)} collective-permute-done((f32[8,2,128,128]{3,2,0,1:T(8,128)}, f32[8,2,128,128]{3,2,0,1:T(8,128)S(1)}, u32[]{:S(2)}, u32[]{:S(2)}) %collective-permute-start.2) | collective-permute-done | bytes 1048608 | tf_op jit(solution)/shard_map/ppermute | solution.py:14
  (266 shorter events, 163.1 us)
Async XLA Ops:
  135.9 91.7 %all-to-all-start = ((bf16[8,1,2,2,128,128]{5,4,3,2,1,0:T(8,128)(2,1)}), bf16[8,1,2,2,128,128]{5,4,3,2,1,0:T(8,128)(2,1)S(1)}, u32[]{:S(2)}, u32[]{:S(2)}) async-start(bf16[8,1,2,2,128,128]{5,4,3,2,1,0:T(8,128)(2,1)} %bitcast_select_fusion.3), calls=%async_computation | async-start | bytes 2097152 | tf_op jit(solution)/shard_map/all_to_all | solution.py:148
  227.5 7.4 %copy-start = (bf16[8,2,2,128,128]{4,3,2,1,0:T(8,128)(2,1)}, bf16[8,2,2,128,128]{4,3,2,1,0:T(8,128)(2,1)S(1)}, u32[]{:S(2)}) copy-start(bf16[8,2,2,128,128]{4,3,2,1,0:T(8,128)(2,1)S(1)} %get-tuple-element.37) | copy-start | bytes 3145732
  227.5 38.4 %all-to-all-start.1 = ((bf16[8,1,2,2,128,128]{5,4,3,2,1,0:T(8,128)(2,1)}), bf16[8,1,2,2,128,128]{5,4,3,2,1,0:T(8,128)(2,1)}, u32[]{:S(2)}, u32[]{:S(2)}) async-start(bf16[8,1,2,2,128,128]{5,4,3,2,1,0:T(8,128)(2,1)} %bitcast_select_fusion.2), calls=%async_computation.1 | async-start | bytes 2097152 | tf_op jit(solution)/shard_map/all_to_all | solution.py:148
  261.0 18.3 %collective-permute-start = (f32[8,2,128,128]{3,2,0,1:T(8,128)S(1)}, f32[8,2,128,128]{3,2,0,1:T(8,128)}, u32[]{:S(2)}, u32[]{:S(2)}) collective-permute-start(f32[8,2,128,128]{3,2,0,1:T(8,128)S(1)} %pad_maximum_fusion), channel_id=1, source_target_pairs={{0,8},{8,16},{16,24},{24,32},{32,40},{40,48},{48,56},{56,64},{64,7... | collective-permute-start | bytes 3145736 | tf_op jit(solution)/shard_map/ppermute | solution.py:14
  266.0 44.8 %all-to-all-start.2 = ((bf16[8,1,2,2,128,128]{5,4,3,2,1,0:T(8,128)(2,1)}), bf16[8,1,2,2,128,128]{5,4,3,2,1,0:T(8,128)(2,1)S(1)}, u32[]{:S(2)}, u32[]{:S(2)}) async-start(bf16[8,1,2,2,128,128]{5,4,3,2,1,0:T(8,128)(2,1)} %bitcast_select_fusion.1), calls=%async_computation.2 | async-start | bytes 2097152 | tf_op jit(solution)/shard_map/all_to_all | solution.py:148
  275.1 4.2 %copy-start.2 = (f32[2,128,128]{2,1,0:T(8,128)S(1)}, f32[2,128,128]{2,1,0:T(8,128)}, u32[]{:S(2)}) copy-start(f32[2,128,128]{2,1,0:T(8,128)} %param.8) | copy-start | bytes 393220
  305.9 3.8 copy-start.1
  306.9 18.5 %collective-permute-start.1 = (f32[8,2,128,128]{3,2,0,1:T(8,128)}, f32[8,2,128,128]{3,2,0,1:T(8,128)}, u32[]{:S(2)}, u32[]{:S(2)}) collective-permute-start(f32[8,2,128,128]{3,2,0,1:T(8,128)} %pad_maximum_fusion.1), channel_id=1, source_target_pairs={{0,8},{8,16},{16,24},{24,32},{32,40},{40,48},{48,56},{56,64},{64,7... | collective-permute-start | bytes 3145736 | tf_op jit(solution)/shard_map/ppermute | solution.py:14
  310.8 44.9 %all-to-all-start.3 = ((bf16[8,1,2,2,128,128]{5,4,3,2,1,0:T(8,128)(2,1)}), bf16[8,1,2,2,128,128]{5,4,3,2,1,0:T(8,128)(2,1)S(1)}, u32[]{:S(2)}, u32[]{:S(2)}) async-start(bf16[8,1,2,2,128,128]{5,4,3,2,1,0:T(8,128)(2,1)} %bitcast_select_fusion), calls=%async_computation.3 | async-start | bytes 2097152 | tf_op jit(solution)/shard_map/all_to_all | solution.py:148
  352.9 18.4 %collective-permute-start.2 = (f32[8,2,128,128]{3,2,0,1:T(8,128)}, f32[8,2,128,128]{3,2,0,1:T(8,128)S(1)}, u32[]{:S(2)}, u32[]{:S(2)}) collective-permute-start(f32[8,2,128,128]{3,2,0,1:T(8,128)} %pad_maximum_fusion.2), channel_id=1, source_target_pairs={{0,8},{8,16},{16,24},{24,32},{32,40},{40,48},{48,56},{56,64},{64,7... | collective-permute-start | bytes 3145736 | tf_op jit(solution)/shard_map/ppermute | solution.py:14
where the time goes:
time: 404 us; the launch traced here: 398 us
  local copies, waits for them, and re-layouts  118 us (29%)
  matrix products  99.2 us (25%)
  blocking collectives  98.6 us (24%)
  starting transfers between devices  33.7 us (8%)
  waiting for transfers between devices  25.3 us (6%)
  other arithmetic  21 us (5%)
    gather x96, local copies, waits for them, and re-layouts  101 us
    dot_general x96, matrix products, plane_dot(): jnp.dot(flat, table, precision=lax.Precision.HIGHEST, preferred_element_t...  99.2 us
    all_gather x4, blocking collectives, per_device(): lax.all_gather(listing[None], 'tile', axis=0, tiled=True)  83.4 us
    all_to_all x4, starting transfers between devices, per_device(): lax.all_to_all(outgoing(got_lists, got_counts), 'tile', split_axis=0, con...  28 us
    ppermute x3, waiting for transfers between devices, from_behind(): lax.ppermute(value, axis, [(source, source + steps) for source in range(l...  25.3 us
    all_gather x1, blocking collectives, per_device(): lax.all_gather(count[None], 'tile', axis=0, tiled=True)  15.2 us
    unnamed x23, local copies, waits for them, and re-layouts  8.72 us
  transfers between devices with their start and end apart: 7, of which 3 were waited for; matrix products, arithmetic and copies ran while one was open for 44% of the time, Pallas kernels for 0%

commit v1 on v0

--- a/solution.py
+++ b/solution.py
@@ -6,6 +6,11 @@
 
 STEPS = 4
 fresnel_rate = 0.3
+
+
+def swapped_in(array, axis, along):
+    sent = jnp.stack([array] * lax.axis_size(axis))
+    return jnp.concatenate(lax.all_to_all(sent, axis, 0, 0), axis=along)
 
 
 def from_behind(value, axis, steps):
@@ -143,7 +148,7 @@
             wavefield = wavefield * live
         got_lists, got_counts = (
             lax.all_gather(listing[None], "tile", axis=0, tiled=True),
-            lax.all_gather(count[None], "tile", axis=0, tiled=True),
+            swapped_in(count[None], "tile", 0),
         )
         received = lax.all_to_all(
             outgoing(got_lists, got_counts), "tile", split_axis=0, concat_axis=0, tiled=True

time: 404 us -> 417 us (1.032)
  starting transfers between devices: 33.7 us -> 57.8 us
  blocking collectives: 98.6 us -> 85.2 us
  waiting for transfers between devices: 25.3 us -> 32.5 us
  local copies, waits for them, and re-layouts: 118 us -> 111 us
    all_to_all x0 -> x4, starting transfers between devices: none -> 24.2 us  [swapped_in(): return jnp.concatenate(lax.all_to_all(sent, axis, 0, 0), axis=along)]
    all_to_all x0 -> x4, waiting for transfers between devices: none -> 17.6 us  [swapped_in(): return jnp.concatenate(lax.all_to_all(sent, axis, 0, 0), axis=along)]
    all_gather x1 -> x0, blocking collectives: 15.2 us -> none  [per_device(): lax.all_gather(count[None], 'tile', axis=0, tiled=True)]
    ppermute x3, waiting for transfers between devices: 25.3 us -> 14.9 us  [from_behind(): lax.ppermute(value, axis, [(source, source + steps) for source in range(l...]
    unnamed x23 -> x12, local copies, waits for them, and re-layouts: 8.72 us -> 2 us
    gather x96, local copies, waits for them, and re-layouts: 101 us -> 96.6 us
    another operation x1 -> x5, local copies, waits for them, and re-layouts: 0.01 us -> 4.78 us  [the longest x4 4.78 us: swapped_in(): sent = jnp.stack([array] * lax.axis_size(axis))]
  transfers between devices with their start and end apart: 7 -> 11, of which waited for: 3 -> 4; matrix products, arithmetic and copies ran while one was open for 44% -> 42% of each run, Pallas kernels for 0% -> 0%
where the time goes in v1:
time: 417 us; the launch traced here: 411 us
  local copies, waits for them, and re-layouts  111 us (27%)
  matrix products  99.1 us (24%)
  blocking collectives  85.2 us (20%)
  starting transfers between devices  57.8 us (14%)
  waiting for transfers between devices  32.5 us (8%)
  other arithmetic  22.9 us (5%)
    dot_general x96, matrix products, plane_dot(): jnp.dot(flat, table, precision=lax.Precision.HIGHEST, preferred_element_t...  99.1 us
    gather x96, local copies, waits for them, and re-layouts  96.6 us
    all_gather x4, blocking collectives, per_device(): lax.all_gather(listing[None], 'tile', axis=0, tiled=True)  85.2 us
    all_to_all x4, starting transfers between devices, per_device(): lax.all_to_all(outgoing(got_lists, got_counts), 'tile', split_axis=0, con...  26.7 us
    all_to_all x4, starting transfers between devices, swapped_in(): return jnp.concatenate(lax.all_to_all(sent, axis, 0, 0), axis=along)  24.2 us
    all_to_all x4, waiting for transfers between devices, swapped_in(): return jnp.concatenate(lax.all_to_all(sent, axis, 0, 0), axis=along)  17.6 us
    ppermute x3, waiting for transfers between devices, from_behind(): lax.ppermute(value, axis, [(source, source + steps) for source in range(l...  14.9 us
  transfers between devices with their start and end apart: 11, of which 4 were waited for; matrix products, arithmetic and copies ran while one was open for 42% of the time, Pallas kernels for 0%

profile of v1, /device:TPU:38, one launch (start us, length us, event | category | flops | bytes accessed | tf_op | source)
XLA Modules:
  0.0 410.5 jit_solution(9118509250556246812)
XLA Ops:
  2.6 8.6 %all-to-all-start.6 = ((s32[8,1,1]{2,1,0:T(1,128)}), s32[8,1,1]{2,1,0:T(1,128)S(1)}, u32[]{:S(2)}, u32[]{:S(2)}) async-start(s32[8,1,1]{2,1,0:T(1,128)} %stack.64), calls=%async_computation.6 | async-start | bytes 8192 | tf_op jit(solution)/shard_map/all_to_all | solution.py:13
  12.2 22.1 %all-gather = s32[8,1,3,8]{3,1,2,0:T(1,128)S(1)} all-gather(s32[1,1,3,8]{3,1,2,0:T(1,128)S(1)} %copy.352), channel_id=2, replica_groups=mesh['depth'=32,'tile'=8] {'tile'}, dimensions={0}, use_global_device_ids=true | all-gather | bytes 864 | tf_op jit(solution)/shard_map/all_gather | solution.py:150
  35.6 21.0 %all-gather.1 = s32[8,1,3,8]{3,1,2,0:T(1,128)S(1)} all-gather(s32[1,1,3,8]{3,1,2,0:T(1,128)S(1)} %copy.353), channel_id=3, replica_groups=mesh['depth'=32,'tile'=8] {'tile'}, dimensions={0}, use_global_device_ids=true | all-gather | bytes 864 | tf_op jit(solution)/shard_map/all_gather | solution.py:150
  58.0 21.2 %all-gather.2 = s32[8,1,3,8]{3,1,2,0:T(1,128)S(1)} all-gather(s32[1,1,3,8]{3,1,2,0:T(1,128)S(1)} %copy.354), channel_id=4, replica_groups=mesh['depth'=32,'tile'=8] {'tile'}, dimensions={0}, use_global_device_ids=true | all-gather | bytes 864 | tf_op jit(solution)/shard_map/all_gather | solution.py:150
  81.1 21.0 %all-gather.3 = s32[8,1,3,8]{3,1,2,0:T(1,128)S(1)} all-gather(s32[1,1,3,8]{3,1,2,0:T(1,128)S(1)} %copy.355), channel_id=5, replica_groups=mesh['depth'=32,'tile'=8] {'tile'}, dimensions={0}, use_global_device_ids=true | all-gather | bytes 864 | tf_op jit(solution)/shard_map/all_gather | solution.py:150
  105.7 6.3 %all-to-all-start.4 = ((s32[8,1,1]{2,1,0:T(1,128)}), s32[8,1,1]{2,1,0:T(1,128)S(1)}, u32[]{:S(2)}, u32[]{:S(2)}) async-start(s32[8,1,1]{2,1,0:T(1,128)} %stack.60), calls=%async_computation.4 | async-start | bytes 8192 | tf_op jit(solution)/shard_map/all_to_all | solution.py:13
  112.3 5.8 %all-to-all-done.4 = s32[8,1,1]{2,1,0:T(1,128)S(1)} async-done(((s32[8,1,1]{2,1,0:T(1,128)}), s32[8,1,1]{2,1,0:T(1,128)S(1)}, u32[]{:S(2)}, u32[]{:S(2)}) %all-to-all-start.4) | async-done | bytes 64 | tf_op jit(solution)/shard_map/all_to_all | solution.py:13
  119.4 4.7 %all-to-all-start.2 = ((s32[8,1,1]{2,1,0:T(1,128)}), s32[8,1,1]{2,1,0:T(1,128)S(1)}, u32[]{:S(2)}, u32[]{:S(2)}) async-start(s32[8,1,1]{2,1,0:T(1,128)} %stack.56), calls=%async_computation.2 | async-start | bytes 8192 | tf_op jit(solution)/shard_map/all_to_all | solution.py:13
  124.4 5.9 %all-to-all-done.2 = s32[8,1,1]{2,1,0:T(1,128)S(1)} async-done(((s32[8,1,1]{2,1,0:T(1,128)}), s32[8,1,1]{2,1,0:T(1,128)S(1)}, u32[]{:S(2)}, u32[]{:S(2)}) %all-to-all-start.2) | async-done | bytes 64 | tf_op jit(solution)/shard_map/all_to_all | solution.py:13
  131.5 4.7 %all-to-all-start = ((s32[8,1,1]{2,1,0:T(1,128)}), s32[8,1,1]{2,1,0:T(1,128)S(1)}, u32[]{:S(2)}, u32[]{:S(2)}) async-start(s32[8,1,1]{2,1,0:T(1,128)} %stack.52), calls=%async_computation | async-start | bytes 8192 | tf_op jit(solution)/shard_map/all_to_all | solution.py:13
  136.4 5.9 %all-to-all-done = s32[8,1,1]{2,1,0:T(1,128)S(1)} async-done(((s32[8,1,1]{2,1,0:T(1,128)}), s32[8,1,1]{2,1,0:T(1,128)S(1)}, u32[]{:S(2)}, u32[]{:S(2)}) %all-to-all-start) | async-done | bytes 64 | tf_op jit(solution)/shard_map/all_to_all | solution.py:13
  144.5 24.7 %while.4 = (s32[]{:T(128)}, bf16[2,2,384,384]{3,2,1,0:T(8,128)(2,1)}, s32[8,4]{0,1:T(4,128)S(1)}, bf16[8,2,2,128,128]{4,3,2,1,0:T(8,128)(2,1)S(1)}, s32[]{:T(128)}) while((s32[]{:T(128)}, bf16[2,2,384,384]{3,2,1,0:T(8,128)(2,1)}, s32[8,4]{0,1:T(4,128)S(1)}, bf16[8,2,2,128,128]{4,3,2,1,0:T(8,128)(2,1)S(1)}, s32[]{:T(128)}) %tuple.93), condition=%wide.while_cond, body=%wide.while_body.sunk | while | flops 2 | bytes 262269 | solution.py:98
  145.2 2.4 bitcast_dynamic-update-slice_fusion.8
  148.3 2.4 bitcast_dynamic-update-slice_fusion.8
  151.4 2.4 bitcast_dynamic-update-slice_fusion.8
  154.5 2.4 bitcast_dynamic-update-slice_fusion.8
  157.6 2.4 bitcast_dynamic-update-slice_fusion.8
  160.7 2.4 bitcast_dynamic-update-slice_fusion.8
  163.8 2.4 bitcast_dynamic-update-slice_fusion.8
  166.9 2.4 bitcast_dynamic-update-slice_fusion.8
  170.4 4.9 %all-to-all-start.1 = ((bf16[8,1,2,2,128,128]{5,4,3,2,1,0:T(8,128)(2,1)}), bf16[8,1,2,2,128,128]{5,4,3,2,1,0:T(8,128)(2,1)S(1)}, u32[]{:S(2)}, u32[]{:S(2)}) async-start(bf16[8,1,2,2,128,128]{5,4,3,2,1,0:T(8,128)(2,1)} %bitcast_select_fusion.3), calls=%async_computation.1 | async-start | bytes 2097152 | tf_op jit(solution)/shard_map/all_to_all | solution.py:153
  175.6 24.6 %while.5 = (s32[]{:T(128)}, bf16[2,2,384,384]{3,2,1,0:T(8,128)(2,1)}, s32[8,4]{0,1:T(4,128)S(1)}, bf16[8,2,2,128,128]{4,3,2,1,0:T(8,128)(2,1)S(1)}, s32[]{:T(128)}) while((s32[]{:T(128)}, bf16[2,2,384,384]{3,2,1,0:T(8,128)(2,1)}, s32[8,4]{0,1:T(4,128)S(1)}, bf16[8,2,2,128,128]{4,3,2,1,0:T(8,128)(2,1)S(1)}, s32[]{:T(128)}) %tuple.105), condition=%wide.while_cond.1, body=%wide.while_body.1.sunk | while | flops 2 | bytes 262269 | solution.py:98
  176.2 2.4 bitcast_dynamic-update-slice_fusion.9
  179.3 2.4 bitcast_dynamic-update-slice_fusion.9
  182.4 2.4 bitcast_dynamic-update-slice_fusion.9
  185.5 2.4 bitcast_dynamic-update-slice_fusion.9
  188.5 2.4 bitcast_dynamic-update-slice_fusion.9
  191.6 2.4 bitcast_dynamic-update-slice_fusion.9
  194.7 2.4 bitcast_dynamic-update-slice_fusion.9
  197.8 2.4 bitcast_dynamic-update-slice_fusion.9
  201.3 7.4 %all-to-all-start.3 = ((bf16[8,1,2,2,128,128]{5,4,3,2,1,0:T(8,128)(2,1)}), bf16[8,1,2,2,128,128]{5,4,3,2,1,0:T(8,128)(2,1)S(1)}, u32[]{:S(2)}, u32[]{:S(2)}) async-start(bf16[8,1,2,2,128,128]{5,4,3,2,1,0:T(8,128)(2,1)} %bitcast_select_fusion.2), calls=%async_computation.3 | async-start | bytes 2097152 | tf_op jit(solution)/shard_map/all_to_all | solution.py:153
  239.1 23.7 %while.6 = (s32[]{:T(128)}, bf16[2,2,384,384]{3,2,1,0:T(8,128)(2,1)}, s32[8,4]{0,1:T(4,128)S(1)}, bf16[8,2,2,128,128]{4,3,2,1,0:T(8,128)(2,1)S(1)}, s32[]{:T(128)}) while((s32[]{:T(128)}, bf16[2,2,384,384]{3,2,1,0:T(8,128)(2,1)}, s32[8,4]{0,1:T(4,128)S(1)}, bf16[8,2,2,128,128]{4,3,2,1,0:T(8,128)(2,1)S(1)}, s32[]{:T(128)}) %tuple.106), condition=%wide.while_cond.2, body=%wide.while_body.2.sunk | while | flops 2 | bytes 262269 | solution.py:98
  239.7 2.3 bitcast_dynamic-update-slice_fusion.10
  242.7 2.3 bitcast_dynamic-update-slice_fusion.10
  245.7 2.3 bitcast_dynamic-update-slice_fusion.10
  264.0 7.2 %all-to-all-start.5 = ((bf16[8,1,2,2,128,128]{5,4,3,2,1,0:T(8,128)(2,1)}), bf16[8,1,2,2,128,128]{5,4,3,2,1,0:T(8,128)(2,1)S(1)}, u32[]{:S(2)}, u32[]{:S(2)}) async-start(bf16[8,1,2,2,128,128]{5,4,3,2,1,0:T(8,128)(2,1)} %bitcast_select_fusion.1), calls=%async_computation.5 | async-start | bytes 2097152 | tf_op jit(solution)/shard_map/all_to_all | solution.py:153
  300.4 3.0 collective-permute-start.1
  303.7 24.0 %while.7 = (s32[]{:T(128)}, bf16[2,2,384,384]{3,2,1,0:T(8,128)(2,1)}, s32[8,4]{0,1:T(4,128)S(1)}, bf16[8,2,2,128,128]{4,3,2,1,0:T(8,128)(2,1)S(1)}, s32[]{:T(128)}) while((s32[]{:T(128)}, bf16[2,2,384,384]{3,2,1,0:T(8,128)(2,1)}, s32[8,4]{0,1:T(4,128)S(1)}, bf16[8,2,2,128,128]{4,3,2,1,0:T(8,128)(2,1)S(1)}, s32[]{:T(128)}) %tuple.107), condition=%wide.while_cond.3, body=%wide.while_body.3.sunk | while | flops 2 | bytes 262269 | solution.py:98
  304.3 2.4 bitcast_dynamic-update-slice_fusion.11
  307.3 2.4 bitcast_dynamic-update-slice_fusion.11
  310.3 2.4 bitcast_dynamic-update-slice_fusion.11
  313.3 2.4 bitcast_dynamic-update-slice_fusion.11
  316.3 2.4 bitcast_dynamic-update-slice_fusion.11
  319.3 2.4 bitcast_dynamic-update-slice_fusion.11
  322.3 2.4 bitcast_dynamic-update-slice_fusion.11
  325.3 2.4 bitcast_dynamic-update-slice_fusion.11
  328.8 7.2 %all-to-all-start.7 = ((bf16[8,1,2,2,128,128]{5,4,3,2,1,0:T(8,128)(2,1)}), bf16[8,1,2,2,128,128]{5,4,3,2,1,0:T(8,128)(2,1)S(1)}, u32[]{:S(2)}, u32[]{:S(2)}) async-start(bf16[8,1,2,2,128,128]{5,4,3,2,1,0:T(8,128)(2,1)} %bitcast_select_fusion), calls=%async_computation.7 | async-start | bytes 2097152 | tf_op jit(solution)/shard_map/all_to_all | solution.py:153
  368.1 14.9 %collective-permute-done.2 = f32[8,2,128,128]{3,2,0,1:T(8,128)} collective-permute-done((f32[8,2,128,128]{3,2,0,1:T(8,128)}, f32[8,2,128,128]{3,2,0,1:T(8,128)}, u32[]{:S(2)}, u32[]{:S(2)}) %collective-permute-start.2) | collective-permute-done | bytes 1048608 | tf_op jit(solution)/shard_map/ppermute | solution.py:19
  (270 shorter events, 172.5 us)
Async XLA Ops:
  2.6 101.9 %all-to-all-start.6 = ((s32[8,1,1]{2,1,0:T(1,128)}), s32[8,1,1]{2,1,0:T(1,128)S(1)}, u32[]{:S(2)}, u32[]{:S(2)}) async-start(s32[8,1,1]{2,1,0:T(1,128)} %stack.64), calls=%async_computation.6 | async-start | bytes 8192 | tf_op jit(solution)/shard_map/all_to_all | solution.py:13
  105.7 12.5 %all-to-all-start.4 = ((s32[8,1,1]{2,1,0:T(1,128)}), s32[8,1,1]{2,1,0:T(1,128)S(1)}, u32[]{:S(2)}, u32[]{:S(2)}) async-start(s32[8,1,1]{2,1,0:T(1,128)} %stack.60), calls=%async_computation.4 | async-start | bytes 8192 | tf_op jit(solution)/shard_map/all_to_all | solution.py:13
  119.4 10.8 %all-to-all-start.2 = ((s32[8,1,1]{2,1,0:T(1,128)}), s32[8,1,1]{2,1,0:T(1,128)S(1)}, u32[]{:S(2)}, u32[]{:S(2)}) async-start(s32[8,1,1]{2,1,0:T(1,128)} %stack.56), calls=%async_computation.2 | async-start | bytes 8192 | tf_op jit(solution)/shard_map/all_to_all | solution.py:13
  131.5 10.8 %all-to-all-start = ((s32[8,1,1]{2,1,0:T(1,128)}), s32[8,1,1]{2,1,0:T(1,128)S(1)}, u32[]{:S(2)}, u32[]{:S(2)}) async-start(s32[8,1,1]{2,1,0:T(1,128)} %stack.52), calls=%async_computation | async-start | bytes 8192 | tf_op jit(solution)/shard_map/all_to_all | solution.py:13
  170.4 30.9 %all-to-all-start.1 = ((bf16[8,1,2,2,128,128]{5,4,3,2,1,0:T(8,128)(2,1)}), bf16[8,1,2,2,128,128]{5,4,3,2,1,0:T(8,128)(2,1)S(1)}, u32[]{:S(2)}, u32[]{:S(2)}) async-start(bf16[8,1,2,2,128,128]{5,4,3,2,1,0:T(8,128)(2,1)} %bitcast_select_fusion.3), calls=%async_computation.1 | async-start | bytes 2097152 | tf_op jit(solution)/shard_map/all_to_all | solution.py:153
  201.3 7.4 %copy-start = (bf16[8,1,2,2,128,128]{5,4,3,2,1,0:T(8,128)(2,1)}, bf16[8,1,2,2,128,128]{5,4,3,2,1,0:T(8,128)(2,1)S(1)}, u32[]{:S(2)}) copy-start(bf16[8,1,2,2,128,128]{5,4,3,2,1,0:T(8,128)(2,1)S(1)} %all-to-all-done.1) | copy-start | bytes 3145732
  201.3 62.7 %all-to-all-start.3 = ((bf16[8,1,2,2,128,128]{5,4,3,2,1,0:T(8,128)(2,1)}), bf16[8,1,2,2,128,128]{5,4,3,2,1,0:T(8,128)(2,1)S(1)}, u32[]{:S(2)}, u32[]{:S(2)}) async-start(bf16[8,1,2,2,128,128]{5,4,3,2,1,0:T(8,128)(2,1)} %bitcast_select_fusion.2), calls=%async_computation.3 | async-start | bytes 2097152 | tf_op jit(solution)/shard_map/all_to_all | solution.py:153
  237.0 35.2 %collective-permute-start = (f32[8,2,128,128]{3,2,0,1:T(8,128)}, f32[8,2,128,128]{3,2,0,1:T(8,128)}, u32[]{:S(2)}, u32[]{:S(2)}) collective-permute-start(f32[8,2,128,128]{3,2,0,1:T(8,128)} %pad_maximum_fusion), channel_id=1, source_target_pairs={{0,8},{8,16},{16,24},{24,32},{32,40},{40,48},{48,56},{56,64},{64,7... | collective-permute-start | bytes 3145736 | tf_op jit(solution)/shard_map/ppermute | solution.py:19
  264.0 64.8 %all-to-all-start.5 = ((bf16[8,1,2,2,128,128]{5,4,3,2,1,0:T(8,128)(2,1)}), bf16[8,1,2,2,128,128]{5,4,3,2,1,0:T(8,128)(2,1)S(1)}, u32[]{:S(2)}, u32[]{:S(2)}) async-start(bf16[8,1,2,2,128,128]{5,4,3,2,1,0:T(8,128)(2,1)} %bitcast_select_fusion.1), calls=%async_computation.5 | async-start | bytes 2097152 | tf_op jit(solution)/shard_map/all_to_all | solution.py:153
  272.0 0.9 copy-start.1
  300.4 36.6 %collective-permute-start.1 = (f32[8,2,128,128]{3,2,0,1:T(8,128)}, f32[8,2,128,128]{3,2,0,1:T(8,128)}, u32[]{:S(2)}, u32[]{:S(2)}) collective-permute-start(f32[8,2,128,128]{3,2,0,1:T(8,128)} %pad_maximum_fusion.1), channel_id=1, source_target_pairs={{0,8},{8,16},{16,24},{24,32},{32,40},{40,48},{48,56},{56,64},{64,7... | collective-permute-start | bytes 3145736 | tf_op jit(solution)/shard_map/ppermute | solution.py:19
  328.8 38.4 %all-to-all-start.7 = ((bf16[8,1,2,2,128,128]{5,4,3,2,1,0:T(8,128)(2,1)}), bf16[8,1,2,2,128,128]{5,4,3,2,1,0:T(8,128)(2,1)S(1)}, u32[]{:S(2)}, u32[]{:S(2)}) async-start(bf16[8,1,2,2,128,128]{5,4,3,2,1,0:T(8,128)(2,1)} %bitcast_select_fusion), calls=%async_computation.7 | async-start | bytes 2097152 | tf_op jit(solution)/shard_map/all_to_all | solution.py:153
  364.5 18.5 %collective-permute-start.2 = (f32[8,2,128,128]{3,2,0,1:T(8,128)}, f32[8,2,128,128]{3,2,0,1:T(8,128)}, u32[]{:S(2)}, u32[]{:S(2)}) collective-permute-start(f32[8,2,128,128]{3,2,0,1:T(8,128)} %pad_maximum_fusion.2), channel_id=1, source_target_pairs={{0,8},{8,16},{16,24},{24,32},{32,40},{40,48},{48,56},{56,64},{64,7... | collective-permute-start | bytes 3145736 | tf_op jit(solution)/shard_map/ppermute | solution.py:19
